TPU v7x, 256 devices: a whole 4x4x8 slice. The times are simulated.
256 devices in a mesh: dp: 32 (over y_lo, z, core), ctx: 8 (over x, y_hi).
Axes of the slice: x: 4, y: 4 (y_hi: 2, y_lo: 2; y = y_hi * 2 + y_lo), z: 8, core: 2. Of those that a mesh axis runs over, the one named last changes fastest.
Arguments:
- queries: bfloat16 [32, 1024, 4096], P('dp', 'ctx'), may hold values from -10 to 10
- key_states: bfloat16 [32, 1024, 512], P('dp', 'ctx'), may hold values from -10 to 10
- value_states: bfloat16 [32, 1024, 512], P('dp', 'ctx'), may hold values from -6 to 6
- out_grad: bfloat16 [32, 1024, 4096], P('dp', 'ctx'), may hold values from -6 to 6
- destinations: int32 [32, 256], P('dp', 'ctx'), may hold values from 0 to 31, as said below
- documents: int32 [32, 1024], P('dp'), may hold values from 0 to 512, as said below
Outputs:
- attended: bfloat16 [32, 1024, 4096], P('dp', 'ctx')
- query_grad: bfloat16 [32, 1024, 4096], P('dp', 'ctx')
- key_grad: bfloat16 [32, 1024, 512], P('dp', 'ctx')
- value_grad: bfloat16 [32, 1024, 512], P('dp', 'ctx')
Inputs may be any that keep to these rules, and one draw needn't show every extreme that they name: `destinations`: for each pack and each block of 128 positions, the 32 entries of the block are a permutation of the pack numbers: every block sends exactly one unit to every pack, its own included. `documents`: document numbers start at 0 and never fall along a pack, by one at most from position to position; the longest document of each pack has exactly 512 positions; in pack 0 every other document has one position.
All inputs are finite; a program needn't handle non-finite values.
Results may differ from a plain program's by a relative error of at most 0.019.
Values may be sent and summed in bfloat16 or wider, within the bound.
No kernel may reach another device: no remote copies, remote signals or barrier semaphores. Data moves between devices by JAX's collectives and lax.ppermute only.
A program may use at most 128 MiB of HBM per device.

v0:
```python
import jax
import jax.numpy as jnp
from jax import lax
from jax.experimental import pallas as pl
from jax.experimental.pallas import tpu as pltpu
from jax.sharding import PartitionSpec as P

HEAD_DIM = 128
GROUP = 8
PAIR = 2
UNIT = 4
BLOCK = 128
REACH = 512
HEADS = GROUP * UNIT
ROWS = 2 * HEADS + 2 * UNIT
FAR_BELOW = -1e30
FACTOR = HEAD_DIM**-0.5
LOG2E = 1.4426950408889634

f32 = jnp.float32
bf16 = jnp.bfloat16


def dot(a, b):
    return jnp.dot(a, b, preferred_element_type=f32)


def dot_nt(a, b):
    return lax.dot_general(a, b, (((1,), (1,)), ((), ())), preferred_element_type=f32)


def sending_matrix(slots):
    units = BLOCK // UNIT
    size = PAIR * BLOCK
    unit = lax.broadcasted_iota(jnp.int32, (units, size), 0)
    col = lax.broadcasted_iota(jnp.int32, (units, size), 1)
    spread = ((col % BLOCK) // UNIT == unit).astype(f32).astype(bf16)
    packs = jnp.broadcast_to(slots.astype(f32), (8, units)).astype(bf16)
    where = dot(packs, spread)
    col = lax.broadcasted_iota(jnp.int32, (8, size), 1)
    inner = (col // BLOCK) * UNIT + col % UNIT
    place = where * (PAIR * UNIT) + inner.astype(f32)
    rows = lax.broadcasted_iota(jnp.int32, (size, size), 0).astype(f32)
    return (place[0:1] == rows).astype(f32).astype(bf16)


def returning_matrix(slots):
    units = BLOCK // UNIT
    size = PAIR * BLOCK
    row = lax.broadcasted_iota(jnp.int32, (size, units), 0)
    unit = lax.broadcasted_iota(jnp.int32, (size, units), 1)
    packs = jnp.broadcast_to(slots.astype(f32), (size, units))
    where = jnp.sum(
        jnp.where((row % BLOCK) // UNIT == unit, packs, 0.0), axis=1, keepdims=True
    )
    row = lax.broadcasted_iota(jnp.int32, (size, 1), 0)
    inner = (row // BLOCK) * UNIT + row % UNIT
    place = where * (PAIR * UNIT) + inner.astype(f32)
    cols = lax.broadcasted_iota(jnp.int32, (size, size), 1).astype(f32)
    return (place == cols).astype(f32).astype(bf16)


def slots_of(route):
    return (route % 2) * (BLOCK // UNIT // 2) + route // 2


def send_kernel(
    route_hbm, q_hbm, k_hbm, v_hbm, do_hbm, out_ref, route, q_buf, k_buf, v_buf, do_buf, in_sems
):
    packs = BLOCK // UNIT
    kv_heads = k_buf.shape[1] // HEAD_DIM
    group = GROUP * HEAD_DIM
    cut = 2
    share = kv_heads // cut
    asked = pltpu.make_async_copy(route_hbm, route, in_sems.at[2 * cut + 2])
    asked.start()
    loads = []
    for n in range(cut):
        at = pl.ds(n * share * group, share * group)
        pair = [
            pltpu.make_async_copy(q_hbm.at[0, :, at], q_buf.at[:, at], in_sems.at[2 * n]),
            pltpu.make_async_copy(do_hbm.at[0, :, at], do_buf.at[:, at], in_sems.at[2 * n + 1]),
        ]
        if n == 0:
            pair += [
                pltpu.make_async_copy(k_hbm.at[0], k_buf, in_sems.at[2 * cut]),
                pltpu.make_async_copy(v_hbm.at[0], v_buf, in_sems.at[2 * cut + 1]),
            ]
        for copy in pair:
            copy.start()
        loads.append(pair)
    asked.wait()
    slots = slots_of(route[...])
    move = sending_matrix(slots)
    wide = PAIR * UNIT
    for m in range(kv_heads):
        if m % share == 0:
            for copy in loads[m // share]:
                copy.wait()
        out = out_ref.at[pl.ds(m * packs, packs)]
        for some in range(0, GROUP, 2 * PAIR):
            moved = []
            for h in (some, some + PAIR):
                heads = [pl.ds(m * group + (h + j) * HEAD_DIM, HEAD_DIM) for j in range(PAIR)]
                both = jnp.concatenate(
                    [
                        jnp.concatenate([q_buf[:, at] for at in heads], axis=0),
                        jnp.concatenate([do_buf[:, at] for at in heads], axis=0),
                    ],
                    axis=1,
                )
                moved.append(dot(move, both).reshape(packs, wide, 2 * HEAD_DIM))
            moved = jnp.concatenate(moved, axis=1).astype(bf16)
            low = some * UNIT
            out[:, low : low + 2 * wide, :] = moved[:, :, :HEAD_DIM]
            low = HEADS + some * UNIT
            out[:, low : low + 2 * wide, :] = moved[:, :, HEAD_DIM:]
        at = slice(m * HEAD_DIM, (m + 1) * HEAD_DIM)
        pair = jnp.concatenate([k_buf[:, at], v_buf[:, at]], axis=0)
        out[:, 2 * HEADS :, :] = (
            dot(move, pair).astype(bf16).reshape(packs, wide, HEAD_DIM)
        )


def return_kernel(
    move, in_ref, o_hbm, dq_hbm, dk_hbm, dv_hbm, o_buf, dq_buf, dk_buf, dv_buf, sems
):
    packs = BLOCK // UNIT
    wide = PAIR * UNIT
    kv_heads = dk_buf.shape[1] // HEAD_DIM
    stores = []

    def store(buf, hbm, at):
        copy = pltpu.make_async_copy(buf.at[:, at], hbm.at[0, :, at], sems.at[len(stores)])
        copy.start()
        stores.append(copy)

    for m in range(kv_heads):
        block = in_ref.at[pl.ds(m * packs, packs)]
        kv = block[:, 2 * HEADS :, :].reshape(2 * BLOCK, HEAD_DIM)
        pair = dot(move[...], kv).astype(bf16)
        at = slice(m * HEAD_DIM, (m + 1) * HEAD_DIM)
        dk_buf[:, at] = pair[:BLOCK]
        dv_buf[:, at] = pair[BLOCK:]
        if m == kv_heads - 1:
            every = pl.ds(0, dk_buf.shape[1])
            store(dk_buf, dk_hbm, every)
            store(dv_buf, dv_hbm, every)
        for h in range(0, GROUP, PAIR):
            low = h * UNIT
            o = block[:, low : low + wide, :].reshape(packs * wide, HEAD_DIM)
            low = HEADS + h * UNIT
            dq = block[:, low : low + wide, :].reshape(packs * wide, HEAD_DIM)
            back = dot(move[...], jnp.concatenate([o, dq], axis=1)).astype(bf16)
            for j in range(PAIR):
                first = (m * GROUP + h + j) * HEAD_DIM
                at = slice(first, first + HEAD_DIM)
                rows = slice(j * BLOCK, (j + 1) * BLOCK)
                o_buf[:, at] = back[rows, :HEAD_DIM]
                dq_buf[:, at] = back[rows, HEAD_DIM:]
        at = pl.ds(m * GROUP * HEAD_DIM, GROUP * HEAD_DIM)
        store(o_buf, o_hbm, at)
        store(dq_buf, dq_hbm, at)
    for copy in stores:
        copy.wait()


def prepare_kernel(
    flags, route_ref, docs_ref, other_ref, near_hbm,
    row_docs, col_docs, row_pos, key_pos, apart, together, move,
):
    slots = slots_of(route_ref[...])
    move[...] = returning_matrix(slots)
    r = lax.broadcasted_iota(jnp.int32, (2 * BLOCK, 2 * BLOCK), 0)
    c = lax.broadcasted_iota(jnp.int32, (2 * BLOCK, 2 * BLOCK), 1)

    def place(x):
        inside = x % BLOCK
        unit = (inside % (BLOCK // 2)) // UNIT
        return (inside // (BLOCK // 2)) * BLOCK + unit * 2 * UNIT + (x // BLOCK) * UNIT + x % UNIT

    apart[...] = (place(r) == c).astype(f32).astype(bf16)
    r = lax.broadcasted_iota(jnp.int32, (BLOCK, BLOCK), 0)
    c = lax.broadcasted_iota(jnp.int32, (BLOCK, BLOCK), 1)
    inside = c % (BLOCK // 2)
    to = (inside // UNIT) * 2 * UNIT + (c // (BLOCK // 2)) * UNIT + c % UNIT
    together[...] = (to == r).astype(f32).astype(bf16)
    core = flags[0, 0]
    half = BLOCK // 2

    def key_at(x):
        owner = jnp.where(x < half, core, 1 - core)
        return (2 * ((x % half) // UNIT) + owner) * UNIT + x % UNIT

    def row_at(x):
        return (2 * (x // HEADS) + core) * UNIT + x % UNIT

    key_pos[...] = key_at(lax.broadcasted_iota(jnp.int32, key_pos.shape, 0)).astype(f32)
    row_pos[...] = row_at(lax.broadcasted_iota(jnp.int32, row_pos.shape, 1)).astype(f32)
    docs = jnp.where(flags[0, 1] == 1, docs_ref[...], other_ref[...])
    high = (docs // 32).astype(f32).astype(bf16)
    low = (docs % 32).astype(f32).astype(bf16)
    tall = row_docs.shape[1]
    pos = lax.broadcasted_iota(jnp.int32, (BLOCK, tall), 0)
    to_row = (row_at(lax.broadcasted_iota(jnp.int32, (BLOCK, tall), 1)) == pos).astype(f32).astype(bf16)
    row_docs[...] = dot(high, to_row) * 32 + dot(low, to_row)
    pos = lax.broadcasted_iota(jnp.int32, (BLOCK, BLOCK), 1)
    to_key = (key_at(lax.broadcasted_iota(jnp.int32, (BLOCK, BLOCK), 0)) == pos).astype(f32).astype(bf16)
    for b in range(docs.shape[0]):
        wide_high = jnp.broadcast_to(high[b : b + 1, :], (BLOCK, BLOCK))
        wide_low = jnp.broadcast_to(low[b : b + 1, :], (BLOCK, BLOCK))
        col_docs[b * BLOCK : (b + 1) * BLOCK, :] = (
            dot_nt(to_key, wide_high) * 32 + dot_nt(to_key, wide_low)
        )


def attend_kernel(
    row_docs, col_docs, row_pos, key_pos, apart, together, in_ref, far_ref,
    out_ref, far_grad, near_slopes, near_chances,
    keys, values, keys_t, values_t, dkeys, dvalues, held, pushed, rounded, slopes,
):
    blocks = row_docs.shape[0]
    units = BLOCK // UNIT // 2
    tall = units * HEADS
    back = (REACH + BLOCK - 2) // BLOCK
    at = [slice(b * BLOCK, (b + 1) * BLOCK) for b in range(blocks)]
    mine = [slice(b * units, (b + 1) * units) for b in range(blocks)]
    across = lax.broadcasted_iota(jnp.int32, (BLOCK, BLOCK), 1)
    eye = (lax.broadcasted_iota(jnp.int32, (BLOCK, BLOCK), 0) == across).astype(f32).astype(bf16)

    for b in range(blocks):
        kv = jnp.concatenate(
            [
                in_ref[mine[b], 2 * HEADS :, :].reshape(BLOCK, HEAD_DIM),
                far_ref[mine[b], :, :].reshape(BLOCK, HEAD_DIM),
            ],
            axis=0,
        )
        kv = dot(apart[...], kv)
        keys[at[b], :] = kv[:BLOCK].astype(bf16)
        values[at[b], :] = kv[BLOCK:].astype(bf16)
        keys_t[:, at[b]] = dot_nt(eye, keys[at[b], :]).astype(bf16)
        values_t[:, at[b]] = dot_nt(eye, values[at[b], :]).astype(bf16)
    dkeys[...] = jnp.zeros_like(dkeys)
    dvalues[...] = jnp.zeros_like(dvalues)
    half = BLOCK // 2
    near = [slice(b * BLOCK, b * BLOCK + half) for b in range(blocks)]
    other = [slice(b * BLOCK + half, (b + 1) * BLOCK) for b in range(blocks)]
    firsts = near_firsts(blocks)

    def scores_of(b):
        low = max(0, b - back)
        q = in_ref[mine[b], 0:HEADS, :].reshape(tall, HEAD_DIM)
        docs = row_docs[b : b + 1, :]
        row_max = jnp.full((8, tall), FAR_BELOW, f32)
        for n in range(b + 1 - low):
            scores = dot_nt(keys[at[low + n], :], q)
            allowed = col_docs[at[low + n], 0:1] == docs
            if low + n == b:
                allowed = allowed & (key_pos[:, 0:1] <= row_pos[0:1, :])
            scores = jnp.where(allowed, scores, FAR_BELOW)
            held[b % 2, at[n], :] = scores
            row_max = jnp.maximum(row_max, jnp.max(scores.reshape(BLOCK // 8, 8, tall), axis=0))
        return jnp.max(row_max, axis=0, keepdims=True)

    def weights_of(b, row_max):
        low = max(0, b - back)
        do = in_ref[mine[b], HEADS : 2 * HEADS, :].reshape(tall, HEAD_DIM)
        weight_sum = jnp.zeros((8, tall), f32)
        row_dot = jnp.zeros((8, tall), f32)
        for n in range(b + 1 - low):
            pushes = dot_nt(values[at[low + n], :], do)
            pushed[b % 2, at[n], :] = pushes
            weights = jnp.exp2((held[b % 2, at[n], :] - row_max) * (FACTOR * LOG2E))
            held[b % 2, at[n], :] = weights
            weight_sum = weight_sum + jnp.sum(weights.reshape(BLOCK // 8, 8, tall), axis=0)
            row_dot = row_dot + jnp.sum((weights * pushes).reshape(BLOCK // 8, 8, tall), axis=0)
        inverse = 1.0 / jnp.sum(weight_sum, axis=0, keepdims=True)
        return inverse, jnp.sum(row_dot, axis=0, keepdims=True) * inverse

    def grads_of(b, inverse, row_dot):
        low = max(0, b - back)
        seen = slice(low * BLOCK, (b + 1) * BLOCK)
        count = b + 1 - low
        slot = b % 2
        q = in_ref[mine[b], 0:HEADS, :].reshape(tall, HEAD_DIM)
        do = in_ref[mine[b], HEADS : 2 * HEADS, :].reshape(tall, HEAD_DIM)
        for n in range(count):
            chances = held[slot, at[n], :] * inverse
            slope = (chances * (pushed[slot, at[n], :] - row_dot)).astype(bf16)
            chances = chances.astype(bf16)
            rounded[slot, at[n], :] = chances
            slopes[slot, at[n], :] = slope
            mine_at = slice(firsts[b] + n * half, firsts[b] + (n + 1) * half)
            near_slopes[mine_at, :] = slope[:half]
            near_chances[mine_at, :] = chances[:half]
        chances = rounded.at[slot, pl.ds(0, count * BLOCK), :]
        slope = slopes.at[slot, pl.ds(0, count * BLOCK), :]
        out_t = dot(values_t[:, seen], chances[...]).astype(bf16)
        dq_t = (dot(keys_t[:, seen], slope[...]) * FACTOR).astype(bf16)
        seen = slice(low * half, (b + 1) * half)
        slope = jnp.concatenate([slopes[slot, other[n], :] for n in range(count)], axis=0)
        chances = jnp.concatenate([rounded[slot, other[n], :] for n in range(count)], axis=0)
        dkeys[seen, :] += dot(slope, q)
        dvalues[seen, :] += dot(chances, do)
        out_ref[mine[b], 0:HEADS, :] = out_t.T.reshape(units, HEADS, HEAD_DIM)
        out_ref[mine[b], HEADS : 2 * HEADS, :] = dq_t.T.reshape(units, HEADS, HEAD_DIM)

    row_max = scores_of(0)
    state = weights_of(0, row_max)
    row_max = scores_of(1)
    for b in range(blocks):
        after = weights_of(b + 1, row_max) if b + 1 < blocks else None
        grads_of(b, *state)
        row_max = scores_of(b + 2) if b + 2 < blocks else None
        state = after

    write_grads(together, dkeys, dvalues, far_grad)


def near_firsts(blocks):
    back = (REACH + BLOCK - 2) // BLOCK
    firsts = [0]
    for b in range(blocks):
        firsts.append(firsts[-1] + (min(b, back) + 1) * (BLOCK // 2))
    return firsts


def write_grads(together, dkeys, dvalues, grad):
    half = BLOCK // 2
    for b in range(dkeys.shape[0] // half):
        at = slice(b * half, (b + 1) * half)
        pair = jnp.concatenate(
            [(dkeys[at, :] * FACTOR).astype(bf16), dvalues[at, :].astype(bf16)], axis=0
        )
        units = half // UNIT
        grad[b * units : (b + 1) * units, :, :] = (
            dot(together[...], pair).astype(bf16).reshape(units, 2 * UNIT, HEAD_DIM)
        )


def near_kernel(together, in_ref, near_slopes, near_chances, near_grad, dkeys, dvalues):
    half = BLOCK // 2
    units = half // UNIT
    blocks = in_ref.shape[0] // units
    firsts = near_firsts(blocks)
    dkeys[...] = jnp.zeros_like(dkeys)
    dvalues[...] = jnp.zeros_like(dvalues)
    for b in range(blocks):
        mine = slice(b * units, (b + 1) * units)
        q = in_ref[mine, 0:HEADS, :].reshape(units * HEADS, HEAD_DIM)
        do = in_ref[mine, HEADS : 2 * HEADS, :].reshape(units * HEADS, HEAD_DIM)
        rows = slice(firsts[b], firsts[b + 1])
        seen = slice((b + 1) * half - (firsts[b + 1] - firsts[b]), (b + 1) * half)
        dkeys[seen, :] += dot(near_slopes[rows, :], q)
        dvalues[seen, :] += dot(near_chances[rows, :], do)
    write_grads(together, dkeys, dvalues, near_grad)


def local(queries, key_states, value_states, out_grad, destinations, documents):
    contexts = lax.axis_size("ctx")
    pairs = lax.axis_size("pair")
    packs = 2 * pairs
    kv_heads = key_states.shape[2] // HEAD_DIM
    swap = [(0, 1), (1, 0)]
    core = lax.axis_index("core")

    shape = jax.ShapeDtypeStruct
    whole = pl.BlockSpec(memory_space=pltpu.VMEM)
    away = pl.BlockSpec(memory_space=pl.ANY)

    def stay(x):
        return pltpu.with_memory_space_constraint(x, pltpu.HBM)

    scalars = pl.BlockSpec(memory_space=pltpu.SMEM)
    small = pltpu.CompilerParams(vmem_limit_bytes=40 * 1024 * 1024)
    moved_shape = shape((kv_heads * packs, ROWS, HEAD_DIM), bf16)
    sending = pl.pallas_call(
        send_kernel,
        in_specs=[away] * 5,
        out_specs=whole,
        out_shape=moved_shape,
        scratch_shapes=[
            pltpu.VMEM(destinations.shape, jnp.int32),
            pltpu.VMEM(queries.shape[1:], bf16),
            pltpu.VMEM(key_states.shape[1:], bf16),
            pltpu.VMEM(key_states.shape[1:], bf16),
            pltpu.VMEM(queries.shape[1:], bf16),
            pltpu.SemaphoreType.DMA((2 * kv_heads + 3,)),
        ],
        compiler_params=small,
    )(*map(stay, (destinations, queries, key_states, value_states, out_grad)))

    sending, other_documents = lax.optimization_barrier(
        (sending, lax.ppermute(documents, "core", swap))
    )
    received = lax.all_to_all(sending, ("ctx", "pair"), split_axis=0, concat_axis=0, tiled=True)
    near = received[:, 2 * HEADS :, :]
    far = lax.ppermute(near, "core", swap)

    length = contexts * BLOCK
    tall = GROUP * BLOCK // 2
    flags = jnp.stack([core, (lax.axis_index("ctx") % 2 == core).astype(core.dtype)])
    square = shape((2 * BLOCK, 2 * BLOCK), bf16)
    *prepared, move = pl.pallas_call(
        prepare_kernel,
        in_specs=[scalars, whole, whole, whole, away],
        out_specs=[whole] * 7,
        out_shape=[
            shape((contexts, tall), f32),
            shape((length, HEAD_DIM), f32),
            shape((8, tall), f32),
            shape((BLOCK, HEAD_DIM), f32),
            square,
            shape((BLOCK, BLOCK), bf16),
            square,
        ],
        compiler_params=small,
    )(
        flags.astype(jnp.int32).reshape(1, 2),
        destinations,
        documents.reshape(contexts, BLOCK),
        other_documents.reshape(contexts, BLOCK),
        near,
    )

    grad_shape = shape((kv_heads * packs, 2 * UNIT, HEAD_DIM), bf16)
    window = min(contexts, (REACH + BLOCK - 2) // BLOCK + 1) * BLOCK
    near_shape = shape((near_firsts(contexts)[-1], tall), bf16)
    results, far_grad, near_slopes, near_chances = pl.pallas_call(
        attend_kernel,
        in_specs=[whole] * 8,
        out_specs=[whole] * 4,
        out_shape=[moved_shape, grad_shape, near_shape, near_shape],
        scratch_shapes=[
            pltpu.VMEM((length, HEAD_DIM), bf16),
            pltpu.VMEM((length, HEAD_DIM), bf16),
            pltpu.VMEM((HEAD_DIM, length), bf16),
            pltpu.VMEM((HEAD_DIM, length), bf16),
            pltpu.VMEM((length // 2, HEAD_DIM), f32),
            pltpu.VMEM((length // 2, HEAD_DIM), f32),
            pltpu.VMEM((2, window, tall), f32),
            pltpu.VMEM((2, window, tall), f32),
            pltpu.VMEM((2, window, tall), bf16),
            pltpu.VMEM((2, window, tall), bf16),
        ],
        compiler_params=small,
    )(*prepared, received, far)

    far_grad = lax.ppermute(far_grad, "core", swap)
    near_grad = pl.pallas_call(
        near_kernel,
        in_specs=[whole] * 4,
        out_specs=whole,
        out_shape=grad_shape,
        scratch_shapes=[pltpu.VMEM((length // 2, HEAD_DIM), f32)] * 2,
        compiler_params=small,
    )(prepared[-1], received, near_slopes, near_chances)
    grads = near_grad.astype(f32) + far_grad.astype(f32)
    results = lax.dynamic_update_slice(results, grads.astype(bf16), (0, 2 * HEADS, 0))
    returned = lax.all_to_all(results, ("ctx", "pair"), split_axis=0, concat_axis=0, tiled=True)

    outs = (queries, queries, key_states, value_states)
    return pl.pallas_call(
        return_kernel,
        in_specs=[whole] * 2,
        out_specs=[away] * 4,
        out_shape=[shape(out.shape, bf16) for out in outs],
        scratch_shapes=[pltpu.VMEM(out.shape[1:], bf16) for out in outs]
        + [pltpu.SemaphoreType.DMA((4 * kv_heads + 2,))],
        compiler_params=small,
    )(move, returned)


def solution(mesh):
    split = jax.sharding.Mesh(
        mesh.devices.reshape(-1, 2, mesh.shape["ctx"]), ("pair", "core", "ctx")
    )
    spec = P(("pair", "core"), "ctx", None)
    return jax.shard_map(
        local,
        mesh=split,
        in_specs=(spec, spec, spec, spec, P(("pair", "core"), "ctx"), P(("pair", "core"), None)),
        out_specs=(spec, spec, spec, spec),
        check_vma=False,
    )
```

profile of v0, /device:TPU:1, one launch (start us, length us, event | category | flops | bytes accessed | tf_op | source)
XLA Modules:
  0.0 158.6 jit_solution(11268234998863629701)
XLA Ops:
  0.6 3.3 %collective-permute-start = (s32[1,1024]{1,0:T(1,128)}, s32[1,1024]{1,0:T(1,128)S(1)}, u32[]{:S(2)}, u32[]{:S(2)}) collective-permute-start(s32[1,1024]{1,0:T(1,128)} %param.11), channel_id=1, source_target_pairs={{0,8},{8,0},{1,9},{9,1},{2,10},{10,2},{3,11},{11,3},{4,12},{12,4},... | collective-permute-start | bytes 12296 | tf_op jit(solution)/shard_map/ppermute | solution.py:395
  4.0 2.4 %shard_map.93 = bf16[128,72,128]{2,1,0:T(8,128)(2,1)S(1)} custom-call(s32[1,32]{1,0:T(1,128)} %route_ref.1, bf16[1,128,4096]{2,1,0:T(8,128)(2,1)} %q_hbm.1, bf16[1,128,512]{2,1,0:T(8,128)(2,1)} %k_hbm.1, bf16[1,128,512]{2,1,0:T(8,128)(2,1)} %v_hbm.1, bf16[1,128,4096]{2,1,0:T(8,128)(2,1)} %do_hbm.1), custom_call_target="tpu_custom_call" | custom-call | tf_op jit(solution)/shard_map/pallas_call | solution.py:378
  6.4 0.0 copy-start
  6.4 0.0 copy-start.1
  6.4 0.0 collective-permute-done
  6.4 72.2 %all_to_all.10.in_ref = bf16[128,72,128]{2,1,0:T(8,128)(2,1)S(1)} all-to-all(bf16[128,72,128]{2,1,0:T(8,128)(2,1)S(1)} %shard_map.93), channel_id=1, replica_groups=mesh['pair'=16,'core'=2,'ctx'=8] {'ctx','pair'}, dimensions={0} | all-to-all | bytes 4718592 | tf_op jit(solution)/shard_map/all_to_all | solution.py:397
  78.7 2.6 %collective-permute-start.1 = (bf16[128,8,128]{2,1,0:T(8,128)(2,1)S(1)}, bf16[128,8,128]{2,1,0:T(8,128)(2,1)S(1)}, u32[]{:S(2)}, u32[]{:S(2)}) collective-permute-start(bf16[128,8,128]{2,1,0:T(8,128)(2,1)S(1)} %slice.4.near_hbm), channel_id=1, source_target_pairs={{0,8},{8,0},{1,9},{9,1},{2,10},{10,2},{3,11},{11,3},{4,12},{12,4},... | collective-permute-start | bytes 786440 | tf_op jit(solution)/shard_map/ppermute | solution.py:399
  81.2 0.1 add_bitcast_fusion.flags
  81.3 0.0 copy-done
  81.3 0.0 copy-done.1
  81.3 1.1 shard_map.94
  82.4 0.0 collective-permute-done.1.far_ref
  82.5 8.0 %shard_map.95 = (bf16[128,72,128]{2,1,0:T(8,128)(2,1)S(1)}, bf16[128,8,128]{2,1,0:T(8,128)(2,1)S(1)}, bf16[1920,512]{1,0:T(8,128)(2,1)S(1)}, bf16[1920,512]{1,0:T(8,128)(2,1)S(1)}) custom-call(f32[8,512]{1,0:T(8,128)S(1)} %get-tuple-element.20.row_docs, f32[1024,128]{1,0:T(8,128)S(1)} %get-tuple-element.21.col_docs, f32[8,512]{1,0:T(8,128)S(1)} %get-tuple-element.22.row_pos, ...), custom_call_target="tpu_custom_call" | custom-call | tf_op jit(solution)/shard_map/pallas_call | solution.py:430
  90.5 0.4 collective-permute-start.2
  90.9 1.3 shard_map.96
  92.2 0.0 collective-permute-done.2
  92.2 0.1 fusion
  92.3 64.3 %all_to_all.11.in_ref = bf16[128,72,128]{2,1,0:T(8,128)(2,1)S(1)} all-to-all(bf16[128,72,128]{2,1,0:T(8,128)(2,1)S(1)} %fusion), channel_id=1, replica_groups=mesh['pair'=16,'core'=2,'ctx'=8] {'ctx','pair'}, dimensions={0} | all-to-all | bytes 4718592 | tf_op jit(solution)/shard_map/all_to_all | solution.py:461
  156.6 1.9 %shard_map.97 = (bf16[1,128,4096]{2,1,0:T(8,128)(2,1)}, bf16[1,128,4096]{2,1,0:T(8,128)(2,1)}, bf16[1,128,512]{2,1,0:T(8,128)(2,1)}, bf16[1,128,512]{2,1,0:T(8,128)(2,1)}) custom-call(bf16[256,256]{1,0:T(8,128)(2,1)S(1)} %get-tuple-element.19.move, bf16[128,72,128]{2,1,0:T(8,128)(2,1)S(1)} %all_to_all.11.in_ref), custom_call_target="tpu_custom_call" | custom-call | tf_op jit(solution)/shard_map/pallas_call | solution.py:464
  (1 shorter events, 0.0 us)
Async XLA Ops:
  0.6 5.8 %collective-permute-start = (s32[1,1024]{1,0:T(1,128)}, s32[1,1024]{1,0:T(1,128)S(1)}, u32[]{:S(2)}, u32[]{:S(2)}) collective-permute-start(s32[1,1024]{1,0:T(1,128)} %param.11), channel_id=1, source_target_pairs={{0,8},{8,0},{1,9},{9,1},{2,10},{10,2},{3,11},{11,3},{4,12},{12,4},... | collective-permute-start | bytes 12296 | tf_op jit(solution)/shard_map/ppermute | solution.py:395
  6.4 74.9 %copy-start = (s32[1,1024]{1,0:T(1,128)S(1)}, s32[1,1024]{1,0:T(1,128)}, u32[]{:S(2)}) copy-start(s32[1,1024]{1,0:T(1,128)} %param.11) | copy-start | bytes 12292
  6.4 74.9 %copy-start.1 = (s32[1,32]{1,0:T(1,128)S(1)}, s32[1,32]{1,0:T(1,128)}, u32[]{:S(2)}) copy-start(s32[1,32]{1,0:T(1,128)} %route_ref.1) | copy-start | bytes 388
  78.7 3.8 %collective-permute-start.1 = (bf16[128,8,128]{2,1,0:T(8,128)(2,1)S(1)}, bf16[128,8,128]{2,1,0:T(8,128)(2,1)S(1)}, u32[]{:S(2)}, u32[]{:S(2)}) collective-permute-start(bf16[128,8,128]{2,1,0:T(8,128)(2,1)S(1)} %slice.4.near_hbm), channel_id=1, source_target_pairs={{0,8},{8,0},{1,9},{9,1},{2,10},{10,2},{3,11},{11,3},{4,12},{12,4},... | collective-permute-start | bytes 786440 | tf_op jit(solution)/shard_map/ppermute | solution.py:399
  90.5 1.7 %collective-permute-start.2 = (bf16[128,8,128]{2,1,0:T(8,128)(2,1)S(1)}, bf16[128,8,128]{2,1,0:T(8,128)(2,1)S(1)}, u32[]{:S(2)}, u32[]{:S(2)}) collective-permute-start(bf16[128,8,128]{2,1,0:T(8,128)(2,1)S(1)} %get-tuple-element.29), channel_id=1, source_target_pairs={{0,8},{8,0},{1,9},{9,1},{2,10},{10,2},{3,11},{11,3},{4,12},{12,4},... | collective-permute-start | bytes 786440 | tf_op jit(solution)/shard_map/ppermute | solution.py:450
where the time goes:
time: 159 us
  blocking collectives  136 us (86%)
  Pallas kernels  14.8 us (9%)
  starting transfers between devices  6.3 us (4%)
    all_to_all x1, blocking collectives, local(): lax.all_to_all(sending, ('ctx', 'pair'), split_axis=0, concat_axis=0, til...  72.2 us
    all_to_all x1, blocking collectives, local(): lax.all_to_all(results, ('ctx', 'pair'), split_axis=0, concat_axis=0, til...  64.3 us
    pallas_call x1, Pallas kernels, local(): pl.pallas_call(attend_kernel, in_specs=[whole] * 8, out_specs=[whole] * 4...  8.02 us
    ppermute x1, starting transfers between devices, local(): lax.ppermute(documents, 'core', swap)  3.33 us
  transfers between devices with their start and end apart: 3, of which 0 were waited for; matrix products, arithmetic and copies ran while one was open for 0% of the time, Pallas kernels for 3%

commit v1 on v0

--- a/solution.py
+++ b/solution.py
@@ -253,13 +253,14 @@
         q = in_ref[mine[b], 0:HEADS, :].reshape(tall, HEAD_DIM)
         docs = row_docs[b : b + 1, :]
         row_max = jnp.full((8, tall), FAR_BELOW, f32)
+        every = dot_nt(keys[low * BLOCK : (b + 1) * BLOCK, :], q)
         for n in range(b + 1 - low):
-            scores = dot_nt(keys[at[low + n], :], q)
+            scores = every[at[n], :]
             allowed = col_docs[at[low + n], 0:1] == docs
             if low + n == b:
                 allowed = allowed & (key_pos[:, 0:1] <= row_pos[0:1, :])
             scores = jnp.where(allowed, scores, FAR_BELOW)
-            held[b % 2, at[n], :] = scores
+            held[b % 3, at[n], :] = scores
             row_max = jnp.maximum(row_max, jnp.max(scores.reshape(BLOCK // 8, 8, tall), axis=0))
         return jnp.max(row_max, axis=0, keepdims=True)
 
@@ -268,11 +269,12 @@
         do = in_ref[mine[b], HEADS : 2 * HEADS, :].reshape(tall, HEAD_DIM)
         weight_sum = jnp.zeros((8, tall), f32)
         row_dot = jnp.zeros((8, tall), f32)
+        every = dot_nt(values[low * BLOCK : (b + 1) * BLOCK, :], do)
         for n in range(b + 1 - low):
-            pushes = dot_nt(values[at[low + n], :], do)
-            pushed[b % 2, at[n], :] = pushes
-            weights = jnp.exp2((held[b % 2, at[n], :] - row_max) * (FACTOR * LOG2E))
-            held[b % 2, at[n], :] = weights
+            pushes = every[at[n], :]
+            pushed[b % 3, at[n], :] = pushes
+            weights = jnp.exp2((held[b % 3, at[n], :] - row_max) * (FACTOR * LOG2E))
+            held[b % 3, at[n], :] = weights
             weight_sum = weight_sum + jnp.sum(weights.reshape(BLOCK // 8, 8, tall), axis=0)
             row_dot = row_dot + jnp.sum((weights * pushes).reshape(BLOCK // 8, 8, tall), axis=0)
         inverse = 1.0 / jnp.sum(weight_sum, axis=0, keepdims=True)
@@ -282,7 +284,7 @@
         low = max(0, b - back)
         seen = slice(low * BLOCK, (b + 1) * BLOCK)
         count = b + 1 - low
-        slot = b % 2
+        slot = b % 3
         q = in_ref[mine[b], 0:HEADS, :].reshape(tall, HEAD_DIM)
         do = in_ref[mine[b], HEADS : 2 * HEADS, :].reshape(tall, HEAD_DIM)
         for n in range(count):
@@ -310,9 +312,10 @@
     state = weights_of(0, row_max)
     row_max = scores_of(1)
     for b in range(blocks):
+        later = scores_of(b + 2) if b + 2 < blocks else None
         after = weights_of(b + 1, row_max) if b + 1 < blocks else None
         grads_of(b, *state)
-        row_max = scores_of(b + 2) if b + 2 < blocks else None
+        row_max = later
         state = after
 
     write_grads(together, dkeys, dvalues, far_grad)
@@ -439,10 +442,10 @@
             pltpu.VMEM((HEAD_DIM, length), bf16),
             pltpu.VMEM((length // 2, HEAD_DIM), f32),
             pltpu.VMEM((length // 2, HEAD_DIM), f32),
-            pltpu.VMEM((2, window, tall), f32),
-            pltpu.VMEM((2, window, tall), f32),
-            pltpu.VMEM((2, window, tall), bf16),
-            pltpu.VMEM((2, window, tall), bf16),
+            pltpu.VMEM((3, window, tall), f32),
+            pltpu.VMEM((3, window, tall), f32),
+            pltpu.VMEM((3, window, tall), bf16),
+            pltpu.VMEM((3, window, tall), bf16),
         ],
         compiler_params=small,
     )(*prepared, received, far)

time: 159 us -> 158 us (level)
  no operation moved by 1% of the time
where the time goes in v1:
time: 158 us
  blocking collectives  136 us (86%)
  Pallas kernels  14.3 us (9%)
  starting transfers between devices  6.3 us (4%)
    all_to_all x1, blocking collectives, local(): lax.all_to_all(sending, ('ctx', 'pair'), split_axis=0, concat_axis=0, til...  72.2 us
    all_to_all x1, blocking collectives, local(): lax.all_to_all(results, ('ctx', 'pair'), split_axis=0, concat_axis=0, til...  64.3 us
    pallas_call x1, Pallas kernels, local(): pl.pallas_call(attend_kernel, in_specs=[whole] * 8, out_specs=[whole] * 4...  7.6 us
    ppermute x1, starting transfers between devices, local(): lax.ppermute(documents, 'core', swap)  3.33 us
  transfers between devices with their start and end apart: 3, of which 0 were waited for; matrix products, arithmetic and copies ran while one was open for 0% of the time, Pallas kernels for 3%

profile of v1, /device:TPU:1, one launch (start us, length us, event | category | flops | bytes accessed | tf_op | source)
XLA Modules:
  0.0 158.2 jit_solution(2093419884589568991)
XLA Ops:
  0.6 3.3 %collective-permute-start = (s32[1,1024]{1,0:T(1,128)}, s32[1,1024]{1,0:T(1,128)S(1)}, u32[]{:S(2)}, u32[]{:S(2)}) collective-permute-start(s32[1,1024]{1,0:T(1,128)} %param.11), channel_id=1, source_target_pairs={{0,8},{8,0},{1,9},{9,1},{2,10},{10,2},{3,11},{11,3},{4,12},{12,4},... | collective-permute-start | bytes 12296 | tf_op jit(solution)/shard_map/ppermute | solution.py:398
  4.0 2.4 %shard_map.93 = bf16[128,72,128]{2,1,0:T(8,128)(2,1)S(1)} custom-call(s32[1,32]{1,0:T(1,128)} %route_ref.1, bf16[1,128,4096]{2,1,0:T(8,128)(2,1)} %q_hbm.1, bf16[1,128,512]{2,1,0:T(8,128)(2,1)} %k_hbm.1, bf16[1,128,512]{2,1,0:T(8,128)(2,1)} %v_hbm.1, bf16[1,128,4096]{2,1,0:T(8,128)(2,1)} %do_hbm.1), custom_call_target="tpu_custom_call" | custom-call | tf_op jit(solution)/shard_map/pallas_call | solution.py:381
  6.4 0.0 copy-start
  6.4 0.0 copy-start.1
  6.4 0.0 collective-permute-done
  6.4 72.2 %all_to_all.10.in_ref = bf16[128,72,128]{2,1,0:T(8,128)(2,1)S(1)} all-to-all(bf16[128,72,128]{2,1,0:T(8,128)(2,1)S(1)} %shard_map.93), channel_id=1, replica_groups=mesh['pair'=16,'core'=2,'ctx'=8] {'ctx','pair'}, dimensions={0} | all-to-all | bytes 4718592 | tf_op jit(solution)/shard_map/all_to_all | solution.py:400
  78.7 2.6 %collective-permute-start.1 = (bf16[128,8,128]{2,1,0:T(8,128)(2,1)S(1)}, bf16[128,8,128]{2,1,0:T(8,128)(2,1)S(1)}, u32[]{:S(2)}, u32[]{:S(2)}) collective-permute-start(bf16[128,8,128]{2,1,0:T(8,128)(2,1)S(1)} %slice.4.near_hbm), channel_id=1, source_target_pairs={{0,8},{8,0},{1,9},{9,1},{2,10},{10,2},{3,11},{11,3},{4,12},{12,4},... | collective-permute-start | bytes 786440 | tf_op jit(solution)/shard_map/ppermute | solution.py:402
  81.2 0.1 add_bitcast_fusion.flags
  81.3 0.0 copy-done
  81.3 0.0 copy-done.1
  81.3 1.1 shard_map.94
  82.4 0.0 collective-permute-done.1.far_ref
  82.5 7.6 %shard_map.95 = (bf16[128,72,128]{2,1,0:T(8,128)(2,1)S(1)}, bf16[128,8,128]{2,1,0:T(8,128)(2,1)S(1)}, bf16[1920,512]{1,0:T(8,128)(2,1)S(1)}, bf16[1920,512]{1,0:T(8,128)(2,1)S(1)}) custom-call(f32[8,512]{1,0:T(8,128)S(1)} %get-tuple-element.20.row_docs, f32[1024,128]{1,0:T(8,128)S(1)} %get-tuple-element.21.col_docs, f32[8,512]{1,0:T(8,128)S(1)} %get-tuple-element.22.row_pos, ...), custom_call_target="tpu_custom_call" | custom-call | tf_op jit(solution)/shard_map/pallas_call | solution.py:433
  90.1 0.4 collective-permute-start.2
  90.5 1.3 shard_map.96
  91.8 0.0 collective-permute-done.2
  91.8 0.1 fusion
  91.9 64.3 %all_to_all.11.in_ref = bf16[128,72,128]{2,1,0:T(8,128)(2,1)S(1)} all-to-all(bf16[128,72,128]{2,1,0:T(8,128)(2,1)S(1)} %fusion), channel_id=1, replica_groups=mesh['pair'=16,'core'=2,'ctx'=8] {'ctx','pair'}, dimensions={0} | all-to-all | bytes 4718592 | tf_op jit(solution)/shard_map/all_to_all | solution.py:464
  156.2 1.9 %shard_map.97 = (bf16[1,128,4096]{2,1,0:T(8,128)(2,1)}, bf16[1,128,4096]{2,1,0:T(8,128)(2,1)}, bf16[1,128,512]{2,1,0:T(8,128)(2,1)}, bf16[1,128,512]{2,1,0:T(8,128)(2,1)}) custom-call(bf16[256,256]{1,0:T(8,128)(2,1)S(1)} %get-tuple-element.19.move, bf16[128,72,128]{2,1,0:T(8,128)(2,1)S(1)} %all_to_all.11.in_ref), custom_call_target="tpu_custom_call" | custom-call | tf_op jit(solution)/shard_map/pallas_call | solution.py:467
  (1 shorter events, 0.0 us)
Async XLA Ops:
  0.6 5.8 %collective-permute-start = (s32[1,1024]{1,0:T(1,128)}, s32[1,1024]{1,0:T(1,128)S(1)}, u32[]{:S(2)}, u32[]{:S(2)}) collective-permute-start(s32[1,1024]{1,0:T(1,128)} %param.11), channel_id=1, source_target_pairs={{0,8},{8,0},{1,9},{9,1},{2,10},{10,2},{3,11},{11,3},{4,12},{12,4},... | collective-permute-start | bytes 12296 | tf_op jit(solution)/shard_map/ppermute | solution.py:398
  6.4 74.9 %copy-start = (s32[1,1024]{1,0:T(1,128)S(1)}, s32[1,1024]{1,0:T(1,128)}, u32[]{:S(2)}) copy-start(s32[1,1024]{1,0:T(1,128)} %param.11) | copy-start | bytes 12292
  6.4 74.9 %copy-start.1 = (s32[1,32]{1,0:T(1,128)S(1)}, s32[1,32]{1,0:T(1,128)}, u32[]{:S(2)}) copy-start(s32[1,32]{1,0:T(1,128)} %route_ref.1) | copy-start | bytes 388
  78.7 3.8 %collective-permute-start.1 = (bf16[128,8,128]{2,1,0:T(8,128)(2,1)S(1)}, bf16[128,8,128]{2,1,0:T(8,128)(2,1)S(1)}, u32[]{:S(2)}, u32[]{:S(2)}) collective-permute-start(bf16[128,8,128]{2,1,0:T(8,128)(2,1)S(1)} %slice.4.near_hbm), channel_id=1, source_target_pairs={{0,8},{8,0},{1,9},{9,1},{2,10},{10,2},{3,11},{11,3},{4,12},{12,4},... | collective-permute-start | bytes 786440 | tf_op jit(solution)/shard_map/ppermute | solution.py:402
  90.1 1.7 %collective-permute-start.2 = (bf16[128,8,128]{2,1,0:T(8,128)(2,1)S(1)}, bf16[128,8,128]{2,1,0:T(8,128)(2,1)S(1)}, u32[]{:S(2)}, u32[]{:S(2)}) collective-permute-start(bf16[128,8,128]{2,1,0:T(8,128)(2,1)S(1)} %get-tuple-element.29), channel_id=1, source_target_pairs={{0,8},{8,0},{1,9},{9,1},{2,10},{10,2},{3,11},{11,3},{4,12},{12,4},... | collective-permute-start | bytes 786440 | tf_op jit(solution)/shard_map/ppermute | solution.py:453

commit v2 on v1

--- a/solution.py
+++ b/solution.py
@@ -262,9 +262,10 @@
             scores = jnp.where(allowed, scores, FAR_BELOW)
             held[b % 3, at[n], :] = scores
             row_max = jnp.maximum(row_max, jnp.max(scores.reshape(BLOCK // 8, 8, tall), axis=0))
-        return jnp.max(row_max, axis=0, keepdims=True)
-
-    def weights_of(b, row_max):
+            yield
+        maxima[b] = jnp.max(row_max, axis=0, keepdims=True)
+
+    def weights_of(b):
         low = max(0, b - back)
         do = in_ref[mine[b], HEADS : 2 * HEADS, :].reshape(tall, HEAD_DIM)
         weight_sum = jnp.zeros((8, tall), f32)
@@ -273,14 +274,16 @@
         for n in range(b + 1 - low):
             pushes = every[at[n], :]
             pushed[b % 3, at[n], :] = pushes
-            weights = jnp.exp2((held[b % 3, at[n], :] - row_max) * (FACTOR * LOG2E))
+            weights = jnp.exp2((held[b % 3, at[n], :] - maxima[b]) * (FACTOR * LOG2E))
             held[b % 3, at[n], :] = weights
             weight_sum = weight_sum + jnp.sum(weights.reshape(BLOCK // 8, 8, tall), axis=0)
             row_dot = row_dot + jnp.sum((weights * pushes).reshape(BLOCK // 8, 8, tall), axis=0)
+            yield
         inverse = 1.0 / jnp.sum(weight_sum, axis=0, keepdims=True)
-        return inverse, jnp.sum(row_dot, axis=0, keepdims=True) * inverse
-
-    def grads_of(b, inverse, row_dot):
+        sums[b] = inverse, jnp.sum(row_dot, axis=0, keepdims=True) * inverse
+
+    def grads_of(b):
+        inverse, row_dot = sums[b]
         low = max(0, b - back)
         seen = slice(low * BLOCK, (b + 1) * BLOCK)
         count = b + 1 - low
@@ -296,28 +299,39 @@
             mine_at = slice(firsts[b] + n * half, firsts[b] + (n + 1) * half)
             near_slopes[mine_at, :] = slope[:half]
             near_chances[mine_at, :] = chances[:half]
+            yield
         chances = rounded.at[slot, pl.ds(0, count * BLOCK), :]
         slope = slopes.at[slot, pl.ds(0, count * BLOCK), :]
         out_t = dot(values_t[:, seen], chances[...]).astype(bf16)
+        yield
         dq_t = (dot(keys_t[:, seen], slope[...]) * FACTOR).astype(bf16)
+        yield
         seen = slice(low * half, (b + 1) * half)
         slope = jnp.concatenate([slopes[slot, other[n], :] for n in range(count)], axis=0)
         chances = jnp.concatenate([rounded[slot, other[n], :] for n in range(count)], axis=0)
         dkeys[seen, :] += dot(slope, q)
+        yield
         dvalues[seen, :] += dot(chances, do)
+        yield
         out_ref[mine[b], 0:HEADS, :] = out_t.T.reshape(units, HEADS, HEAD_DIM)
         out_ref[mine[b], HEADS : 2 * HEADS, :] = dq_t.T.reshape(units, HEADS, HEAD_DIM)
 
-    row_max = scores_of(0)
-    state = weights_of(0, row_max)
-    row_max = scores_of(1)
+    maxima, sums = {}, {}
+
+    def together_run(*parts):
+        parts = list(parts)
+        while parts:
+            parts = [part for part in parts if next(part, parts) is None]
+
+    together_run(scores_of(0))
+    together_run(scores_of(1), weights_of(0))
     for b in range(blocks):
-        later = scores_of(b + 2) if b + 2 < blocks else None
-        after = weights_of(b + 1, row_max) if b + 1 < blocks else None
-        grads_of(b, *state)
-        row_max = later
-        state = after
-
+        parts = [grads_of(b)]
+        if b + 1 < blocks:
+            parts.append(weights_of(b + 1))
+        if b + 2 < blocks:
+            parts.append(scores_of(b + 2))
+        together_run(*parts)
     write_grads(together, dkeys, dvalues, far_grad)
 
 

time: 158 us -> 158 us (level)
  no operation moved by 1% of the time
where the time goes in v2:
time: 158 us
  blocking collectives  136 us (86%)
  Pallas kernels  14.1 us (9%)
  starting transfers between devices  6.31 us (4%)
    all_to_all x1, blocking collectives, local(): lax.all_to_all(sending, ('ctx', 'pair'), split_axis=0, concat_axis=0, til...  72.2 us
    all_to_all x1, blocking collectives, local(): lax.all_to_all(results, ('ctx', 'pair'), split_axis=0, concat_axis=0, til...  64.3 us
    pallas_call x1, Pallas kernels, local(): pl.pallas_call(attend_kernel, in_specs=[whole] * 8, out_specs=[whole] * 4...  7.33 us
    ppermute x1, starting transfers between devices, local(): lax.ppermute(documents, 'core', swap)  3.33 us
  transfers between devices with their start and end apart: 3, of which 0 were waited for; matrix products, arithmetic and copies ran while one was open for 0% of the time, Pallas kernels for 3%

profile of v2, /device:TPU:1, one launch (start us, length us, event | category | flops | bytes accessed | tf_op | source)
XLA Modules:
  0.0 158.0 jit_solution(2913356938468648444)
XLA Ops:
  0.6 3.3 %collective-permute-start = (s32[1,1024]{1,0:T(1,128)}, s32[1,1024]{1,0:T(1,128)S(1)}, u32[]{:S(2)}, u32[]{:S(2)}) collective-permute-start(s32[1,1024]{1,0:T(1,128)} %param.11), channel_id=1, source_target_pairs={{0,8},{8,0},{1,9},{9,1},{2,10},{10,2},{3,11},{11,3},{4,12},{12,4},... | collective-permute-start | bytes 12296 | tf_op jit(solution)/shard_map/ppermute | solution.py:412
  4.0 2.4 %shard_map.93 = bf16[128,72,128]{2,1,0:T(8,128)(2,1)S(1)} custom-call(s32[1,32]{1,0:T(1,128)} %route_ref.1, bf16[1,128,4096]{2,1,0:T(8,128)(2,1)} %q_hbm.1, bf16[1,128,512]{2,1,0:T(8,128)(2,1)} %k_hbm.1, bf16[1,128,512]{2,1,0:T(8,128)(2,1)} %v_hbm.1, bf16[1,128,4096]{2,1,0:T(8,128)(2,1)} %do_hbm.1), custom_call_target="tpu_custom_call" | custom-call | tf_op jit(solution)/shard_map/pallas_call | solution.py:395
  6.4 0.0 copy-start
  6.4 0.0 copy-start.1
  6.4 0.0 collective-permute-done
  6.4 72.2 %all_to_all.10.in_ref = bf16[128,72,128]{2,1,0:T(8,128)(2,1)S(1)} all-to-all(bf16[128,72,128]{2,1,0:T(8,128)(2,1)S(1)} %shard_map.93), channel_id=1, replica_groups=mesh['pair'=16,'core'=2,'ctx'=8] {'ctx','pair'}, dimensions={0} | all-to-all | bytes 4718592 | tf_op jit(solution)/shard_map/all_to_all | solution.py:414
  78.7 2.4 %collective-permute-start.1 = (bf16[128,8,128]{2,1,0:T(8,128)(2,1)S(1)}, bf16[128,8,128]{2,1,0:T(8,128)(2,1)S(1)}, u32[]{:S(2)}, u32[]{:S(2)}) collective-permute-start(bf16[128,8,128]{2,1,0:T(8,128)(2,1)S(1)} %slice.4.near_hbm), channel_id=1, source_target_pairs={{0,8},{8,0},{1,9},{9,1},{2,10},{10,2},{3,11},{11,3},{4,12},{12,4},... | collective-permute-start | bytes 786440 | tf_op jit(solution)/shard_map/ppermute | solution.py:416
  81.0 0.1 add_bitcast_fusion.flags
  81.1 0.0 copy-done
  81.1 0.0 copy-done.1
  81.1 1.1 shard_map.94
  82.3 0.0 collective-permute-done.1.far_ref
  82.3 7.3 %shard_map.95 = (bf16[128,72,128]{2,1,0:T(8,128)(2,1)S(1)}, bf16[128,8,128]{2,1,0:T(8,128)(2,1)S(1)}, bf16[1920,512]{1,0:T(8,128)(2,1)S(1)}, bf16[1920,512]{1,0:T(8,128)(2,1)S(1)}) custom-call(f32[8,512]{1,0:T(8,128)S(1)} %get-tuple-element.20.row_docs, f32[1024,128]{1,0:T(8,128)S(1)} %get-tuple-element.21.col_docs, f32[8,512]{1,0:T(8,128)S(1)} %get-tuple-element.22.row_pos, ...), custom_call_target="tpu_custom_call" | custom-call | tf_op jit(solution)/shard_map/pallas_call | solution.py:447
  89.6 0.6 collective-permute-start.2
  90.2 1.3 shard_map.96
  91.5 0.0 collective-permute-done.2
  91.5 0.1 fusion
  91.6 64.3 %all_to_all.11.in_ref = bf16[128,72,128]{2,1,0:T(8,128)(2,1)S(1)} all-to-all(bf16[128,72,128]{2,1,0:T(8,128)(2,1)S(1)} %fusion), channel_id=1, replica_groups=mesh['pair'=16,'core'=2,'ctx'=8] {'ctx','pair'}, dimensions={0} | all-to-all | bytes 4718592 | tf_op jit(solution)/shard_map/all_to_all | solution.py:478
  155.9 1.9 %shard_map.97 = (bf16[1,128,4096]{2,1,0:T(8,128)(2,1)}, bf16[1,128,4096]{2,1,0:T(8,128)(2,1)}, bf16[1,128,512]{2,1,0:T(8,128)(2,1)}, bf16[1,128,512]{2,1,0:T(8,128)(2,1)}) custom-call(bf16[256,256]{1,0:T(8,128)(2,1)S(1)} %get-tuple-element.19.move, bf16[128,72,128]{2,1,0:T(8,128)(2,1)S(1)} %all_to_all.11.in_ref), custom_call_target="tpu_custom_call" | custom-call | tf_op jit(solution)/shard_map/pallas_call | solution.py:481
  (1 shorter events, 0.0 us)
Async XLA Ops:
  0.6 5.8 %collective-permute-start = (s32[1,1024]{1,0:T(1,128)}, s32[1,1024]{1,0:T(1,128)S(1)}, u32[]{:S(2)}, u32[]{:S(2)}) collective-permute-start(s32[1,1024]{1,0:T(1,128)} %param.11), channel_id=1, source_target_pairs={{0,8},{8,0},{1,9},{9,1},{2,10},{10,2},{3,11},{11,3},{4,12},{12,4},... | collective-permute-start | bytes 12296 | tf_op jit(solution)/shard_map/ppermute | solution.py:412
  6.4 74.8 %copy-start = (s32[1,1024]{1,0:T(1,128)S(1)}, s32[1,1024]{1,0:T(1,128)}, u32[]{:S(2)}) copy-start(s32[1,1024]{1,0:T(1,128)} %param.11) | copy-start | bytes 12292
  6.4 74.7 %copy-start.1 = (s32[1,32]{1,0:T(1,128)S(1)}, s32[1,32]{1,0:T(1,128)}, u32[]{:S(2)}) copy-start(s32[1,32]{1,0:T(1,128)} %route_ref.1) | copy-start | bytes 388
  78.7 3.6 %collective-permute-start.1 = (bf16[128,8,128]{2,1,0:T(8,128)(2,1)S(1)}, bf16[128,8,128]{2,1,0:T(8,128)(2,1)S(1)}, u32[]{:S(2)}, u32[]{:S(2)}) collective-permute-start(bf16[128,8,128]{2,1,0:T(8,128)(2,1)S(1)} %slice.4.near_hbm), channel_id=1, source_target_pairs={{0,8},{8,0},{1,9},{9,1},{2,10},{10,2},{3,11},{11,3},{4,12},{12,4},... | collective-permute-start | bytes 786440 | tf_op jit(solution)/shard_map/ppermute | solution.py:416
  89.6 1.9 %collective-permute-start.2 = (bf16[128,8,128]{2,1,0:T(8,128)(2,1)S(1)}, bf16[128,8,128]{2,1,0:T(8,128)(2,1)S(1)}, u32[]{:S(2)}, u32[]{:S(2)}) collective-permute-start(bf16[128,8,128]{2,1,0:T(8,128)(2,1)S(1)} %get-tuple-element.29), channel_id=1, source_target_pairs={{0,8},{8,0},{1,9},{9,1},{2,10},{10,2},{3,11},{11,3},{4,12},{12,4},... | collective-permute-start | bytes 786440 | tf_op jit(solution)/shard_map/ppermute | solution.py:467
